TPU v7x, 32 devices: a whole 2x2x4 slice. The times are simulated.
32 devices in a mesh: cols: 8 (over z, x), mem: 4 (over y, core).
Axes of the slice: x: 2, y: 2, z: 4, core: 2. Of those that a mesh axis runs over, the one named last changes fastest.
Arguments:
- column_profiles: bfloat16 [128, 100, 512], P('cols', None, 'mem'), may hold values from -6 to 6
- w_in: bfloat16 [100, 256], replicated, may hold values from -0.625 to 0.625
- w_depth: float32 [3, 256], replicated, may hold values from -3 to 3
- w_out: bfloat16 [256, 100], replicated, may hold values from -0.375 to 0.375
- obs_op: float32 [100, 16], replicated, may hold values from -0.625 to 0.625
- foot: int32 [1024, 4], P('cols'), may hold values from -1 to 15, as said below
- owner: int32 [1024, 1], P('cols'), may hold values from 0 to 7; in each aligned block of 128 rows (0 to 127, 128 to 255, ...) at most 32 rows name the same one
- obs: float32 [1024, 16], P('cols'), may hold values from -6 to 6
- rinv: float32 [1024, 16], P('cols'), may hold values from 0.5 to 4
- inflation: float32 [8], P('cols'), may hold values from 0.5 to 2
Outputs:
- analysis: bfloat16 [128, 100, 512], P('cols', None, 'mem')
Inputs may be any that keep to these rules, and one draw needn't show every extreme that they name: `foot`: the first slot of every batch is a column of its source; other slots are a column or -1. Among the 128 batches of one index of cols, no owner appears more than 32 times.
All inputs are finite; a program needn't handle non-finite values.
Results may differ from a plain program's by a relative error of at most 0.01.
Values may be sent and summed in bfloat16 or wider, within the bound.
A program may use at most 64 MiB of HBM per device.

v0:
```python
import functools
import math

import jax
import jax.numpy as jnp
from jax import lax
from jax.experimental import pallas as pl
from jax.experimental.pallas import tpu as pltpu
from jax.sharding import PartitionSpec as P

TOP = lax.Precision.HIGHEST
F32 = jnp.float32
MESH = pl.DeviceIdType.MESH
VMEM = pl.BlockSpec(memory_space=pltpu.VMEM)


def remote(src, dst, send, recv, where):
    return pltpu.make_async_remote_copy(
        src_ref=src, dst_ref=dst, send_sem=send, recv_sem=recv,
        device_id=where, device_id_type=MESH,
    )


def mem_peers():
    m = lax.axis_index("mem")
    far = lax.rem(m + 2, 4)
    near = m + 1 - 2 * lax.rem(m, 2)
    return m, far, near


def edge_kernel(n_cols, first_ref, last_ref, factor_ref, low_ref, high_ref, factors_ref,
                low_buf, high_buf, factor_buf, edge_send, edge_recv, f_send, f_recv):
    c = lax.axis_index("cols")
    barrier = pltpu.get_barrier_semaphore()
    for d in range(1, n_cols):
        pl.semaphore_signal(barrier, inc=1, device_id={"cols": lax.rem(c + d, n_cols)}, device_id_type=MESH)
    pl.semaphore_wait(barrier, n_cols - 1)
    up = remote(last_ref, low_buf, edge_send.at[0], edge_recv.at[0], {"cols": lax.rem(c + 1, n_cols)})
    down = remote(first_ref, high_buf, edge_send.at[1], edge_recv.at[1], {"cols": lax.rem(c + n_cols - 1, n_cols)})
    up.start()
    down.start()
    copies = []
    for d in range(1, n_cols):
        copy = remote(factor_ref, factor_buf.at[d - 1], f_send.at[d - 1], f_recv.at[d - 1],
                      {"cols": lax.rem(c + d, n_cols)})
        copy.start()
        copies.append(copy)
    factors_ref[c] = factor_ref[...]
    for d in range(1, n_cols):
        copies[d - 1].wait()
        factors_ref[lax.rem(c + n_cols - d, n_cols)] = factor_buf[d - 1]
    up.wait()
    down.wait()
    low_ref[...] = jnp.where(c > 0, low_buf[...].astype(F32), 0.0).astype(low_ref.dtype)
    high_ref[...] = jnp.where(c < n_cols - 1, high_buf[...].astype(F32), 0.0).astype(high_ref.dtype)


def exchange_edges(first, last, factor, n_cols):
    count = n_cols - 1
    return pl.pallas_call(
        functools.partial(edge_kernel, n_cols),
        out_shape=(
            jax.ShapeDtypeStruct(first.shape, first.dtype),
            jax.ShapeDtypeStruct(first.shape, first.dtype),
            jax.ShapeDtypeStruct((n_cols,) + factor.shape, factor.dtype),
        ),
        in_specs=[VMEM] * 3,
        out_specs=(VMEM,) * 3,
        scratch_shapes=[
            pltpu.VMEM(first.shape, first.dtype),
            pltpu.VMEM(first.shape, first.dtype),
            pltpu.VMEM((count,) + factor.shape, factor.dtype),
            pltpu.SemaphoreType.DMA((2,)),
            pltpu.SemaphoreType.DMA((2,)),
            pltpu.SemaphoreType.DMA((count,)),
            pltpu.SemaphoreType.DMA((count,)),
        ],
        compiler_params=pltpu.CompilerParams(collective_id=0, has_side_effects=True, vmem_limit_bytes=16 << 20),
    )(first, last, factor)


def mem_kernel(seen_ref, sums_ref, all_ref, total_ref, seen_buf, sums_buf, send, recv):
    m, far, near = mem_peers()
    barrier = pltpu.get_barrier_semaphore()
    for peer in (far, near):
        pl.semaphore_signal(barrier, inc=1, device_id={"mem": peer}, device_id_type=MESH)
    pl.semaphore_wait(barrier, 2)
    copies = []
    for i, (src, buf) in enumerate(((sums_ref, sums_buf), (seen_ref, seen_buf))):
        a = remote(src, buf.at[0], send.at[i, 0], recv.at[i, 0], {"mem": far})
        b = remote(src, buf.at[1], send.at[i, 1], recv.at[i, 1], {"mem": near})
        a.start()
        b.start()
        copies.append((a, b))
    thirds = []
    for i, buf in enumerate((sums_buf, seen_buf)):
        copies[i][0].wait()
        t = remote(buf.at[0], buf.at[2], send.at[i, 2], recv.at[i, 2], {"mem": near})
        t.start()
        thirds.append(t)
    all_ref[m] = seen_ref[...]
    all_ref[far] = seen_buf[0]
    for i in range(2):
        copies[i][1].wait()
        thirds[i].wait()
    total_ref[...] = (sums_ref[...] + sums_buf[0]) + (sums_buf[1] + sums_buf[2])
    all_ref[near] = seen_buf[1]
    all_ref[lax.rem(near + 2, 4)] = seen_buf[2]


def exchange_mem(seen, sums):
    return pl.pallas_call(
        mem_kernel,
        out_shape=(
            jax.ShapeDtypeStruct((4,) + seen.shape, F32),
            jax.ShapeDtypeStruct(sums.shape, F32),
        ),
        in_specs=[VMEM] * 2,
        out_specs=(VMEM,) * 2,
        scratch_shapes=[
            pltpu.VMEM((3,) + seen.shape, F32),
            pltpu.VMEM((3,) + sums.shape, F32),
            pltpu.SemaphoreType.DMA((2, 3)),
            pltpu.SemaphoreType.DMA((2, 3)),
        ],
        compiler_params=pltpu.CompilerParams(collective_id=1, has_side_effects=True, vmem_limit_bytes=16 << 20),
    )(seen, sums)


def gram_kernel(n_cols, part_ref, vec_ref, gram_ref, total_ref, rbuf, vbuf, gbuf,
                r_send, r_recv, v_send, v_recv, g_send, g_recv,
                a_send, a_recv, b_send, b_recv, t_send, t_recv):
    c = lax.axis_index("cols")
    m, far, near = mem_peers()
    barrier = pltpu.get_barrier_semaphore()
    for d in range(1, n_cols):
        pl.semaphore_signal(barrier, inc=1, device_id={"cols": lax.rem(c + d, n_cols)}, device_id_type=MESH)
    for peer in (far, near):
        pl.semaphore_signal(barrier, inc=1, device_id={"mem": peer}, device_id_type=MESH)
    pl.semaphore_wait(barrier, n_cols + 1)
    rows, vecs = [], []
    for d in range(1, n_cols):
        peer = lax.rem(c + d, n_cols)
        copy = remote(part_ref.at[peer], rbuf.at[d - 1], r_send.at[d - 1], r_recv.at[d - 1], {"cols": peer})
        copy.start()
        rows.append(copy)
    for d in range(1, n_cols):
        peer = lax.rem(c + d, n_cols)
        copy = remote(vec_ref, vbuf.at[d - 1], v_send.at[d - 1], v_recv.at[d - 1], {"cols": peer})
        copy.start()
        vecs.append(copy)
    total = part_ref[c]
    for d in range(1, n_cols):
        rows[d - 1].wait()
        total = total + rbuf[d - 1]
    gbuf[m, c] = total
    spread_out = []
    for d in range(1, n_cols):
        copy = remote(gbuf.at[m, c], gbuf.at[m, c], g_send.at[d - 1], g_recv.at[d - 1],
                      {"cols": lax.rem(c + d, n_cols)})
        copy.start()
        spread_out.append(copy)
    pairs = []
    for d in range(n_cols):
        held = lax.rem(c + n_cols - d, n_cols)
        if d > 0:
            spread_out[d - 1].wait_recv()
        a = remote(gbuf.at[m, held], gbuf.at[m, held], a_send.at[d], a_recv.at[d], {"mem": far})
        b = remote(gbuf.at[m, held], gbuf.at[m, held], b_send.at[d], b_recv.at[d], {"mem": near})
        a.start()
        b.start()
        pairs.append((a, b))
    thirds = []
    for d in range(n_cols):
        held = lax.rem(c + n_cols - d, n_cols)
        pairs[d][0].wait_recv()
        t = remote(gbuf.at[far, held], gbuf.at[far, held], t_send.at[d], t_recv.at[d], {"mem": near})
        t.start()
        thirds.append(t)
    whole = vec_ref[...]
    for d in range(1, n_cols):
        vecs[d - 1].wait()
        whole = whole + vbuf[d - 1]
    total_ref[...] = whole
    for d in range(n_cols):
        pairs[d][1].wait_recv()
        thirds[d].wait_recv()
    for d in range(1, n_cols):
        spread_out[d - 1].wait_send()
    for d in range(n_cols):
        pairs[d][0].wait_send()
        pairs[d][1].wait_send()
        thirds[d].wait_send()
    gram_ref[...] = gbuf[...]


def exchange_gram(part, vec, n_cols):
    count = n_cols - 1
    dma = pltpu.SemaphoreType.DMA
    slab = part.shape[1:]
    return pl.pallas_call(
        functools.partial(gram_kernel, n_cols),
        out_shape=(
            jax.ShapeDtypeStruct((4, n_cols) + slab, F32),
            jax.ShapeDtypeStruct(vec.shape, F32),
        ),
        in_specs=[VMEM] * 2,
        out_specs=(VMEM,) * 2,
        scratch_shapes=[
            pltpu.VMEM((count,) + slab, F32),
            pltpu.VMEM((count,) + vec.shape, F32),
            pltpu.VMEM((4, n_cols) + slab, F32),
        ] + [dma((count,))] * 6 + [dma((n_cols,))] * 6,
        compiler_params=pltpu.CompilerParams(collective_id=2, has_side_effects=True, vmem_limit_bytes=16 << 20),
    )(part, vec)


def lane_copy(x, j):
    return jnp.take_along_axis(x, jnp.full(x.shape, j, jnp.int32), axis=1)


def eliminate(block, width):
    lane = lax.broadcasted_iota(jnp.int32, (8, width), 1)
    sub = lax.broadcasted_iota(jnp.int32, (8, width), 0)
    for p in range(width // 8):
        row = block[p]
        base = 8 * p
        cols = [lane_copy(row, base + k) for k in range(8)]
        recips, tops = [], []
        for j in range(8):
            recip = 1.0 / cols[j][j:j + 1]
            mult = jnp.where(sub > j, cols[j] * recip, 0.0)
            top = {}
            for k in range(j + 1, 8):
                top[k] = cols[k][j:j + 1]
                cols[k] = cols[k] - mult * top[k]
            recips.append(recip)
            tops.append(top)
            row = jnp.where((lane == base + j) & (sub > j), -mult, row - mult * row[j:j + 1])
        block[p] = row
        for q in range(p + 1, width // 8):
            x = block[q]
            below = [lane_copy(x, base + k) for k in range(8)]
            for j in range(8):
                mult = below[j] * recips[j]
                for k in range(j + 1, 8):
                    below[k] = below[k] - mult * tops[j][k]
                x = jnp.where(lane == base + j, -mult, x - mult * row[j:j + 1])
            block[q] = x
    return block


def factor_kernel(scale, first_ref, gram_ref, vec_ref, mix_ref, w_ref):
    width = 128
    order = gram_ref.shape[0]
    blocks = order // width
    w_ref[...] = gram_ref[...]
    lane = lax.broadcasted_iota(jnp.int32, (8, width), 1)
    sub = lax.broadcasted_iota(jnp.int32, (8, width), 0)

    def step(b, carry):
        o = pl.multiple_of(b * width, width)
        block = [
            w_ref[pl.ds(o + 8 * i, 8), pl.ds(o, width)] + jnp.where((lane == sub + 8 * i) , 1.0, 0.0)
            for i in range(width // 8)
        ]
        block = eliminate(block, width)
        rows = []
        for i in range(width // 8):
            diag = lane == sub + 8 * i
            root = lax.rsqrt(jnp.sum(jnp.where(diag, block[i], 0.0), axis=1, keepdims=True))
            rows.append(jnp.where(diag, root, jnp.where(lane < sub + 8 * i, block[i] * root, 0.0)))
        inverse = jnp.concatenate(rows, axis=0)
        solved = jnp.dot(inverse, w_ref[pl.ds(o, width), :], precision=TOP, preferred_element_type=F32)
        w_ref[pl.ds(o, width), :] = solved
        w_ref[pl.ds(o, width), pl.ds(o, width)] = inverse

        def update(t, inner):
            u = pl.multiple_of(t * width, width)
            upper = w_ref[pl.ds(o, width), pl.ds(u, width)]
            product = lax.dot_general(
                upper, w_ref[pl.ds(o, width), :], (((0,), (0,)), ((), ())),
                precision=TOP, preferred_element_type=F32,
            )
            w_ref[pl.ds(u, width), pl.ds(o, width)] = jnp.zeros((width, width), F32)
            w_ref[pl.ds(u, width), :] -= product
            return inner

        lax.fori_loop(b + 1, blocks, update, 0)
        return carry

    lax.fori_loop(0, blocks, step, 0)
    row_id = lax.broadcasted_iota(jnp.int32, (order, order), 0)
    col_id = lax.broadcasted_iota(jnp.int32, (order, order), 1)
    chol_inverse = jnp.where(row_id >= col_id, w_ref[...], 0.0)
    w_ref[...] = chol_inverse
    half = jnp.sum(chol_inverse * vec_ref[...], axis=1, keepdims=True)
    weights = jnp.sum(chol_inverse * half, axis=0, keepdims=True)
    mine = w_ref[pl.ds(pl.multiple_of(first_ref[0] * width, width), mix_ref.shape[0]), :]
    mix_ref[...] = (weights * scale + mine).astype(mix_ref.dtype)


def factor(first, gram, vec, rows, scale):
    order = gram.shape[0]
    return pl.pallas_call(
        functools.partial(factor_kernel, scale),
        out_shape=jax.ShapeDtypeStruct((rows, order), jnp.bfloat16),
        in_specs=[pl.BlockSpec(memory_space=pltpu.SMEM), VMEM, VMEM],
        out_specs=VMEM,
        scratch_shapes=[pltpu.VMEM((order, order), F32)],
        compiler_params=pltpu.CompilerParams(vmem_limit_bytes=32 << 20),
        cost_estimate=pl.CostEstimate(flops=40_000_000_000, bytes_accessed=1 << 22, transcendentals=0),
    )(first, gram, vec)


def body(column_profiles, w_in, w_depth, w_out, obs_op, foot, owner, obs, rinv, inflation):
    n_cols = lax.axis_size("cols")
    n_mem = lax.axis_size("mem")
    col_dev, channels, mem_dev = column_profiles.shape
    n_obs = obs.shape[1]
    members = mem_dev * n_mem
    direct = n_cols <= 8 and n_mem == 4
    scale = 1.0 / math.sqrt(members - 1)

    hidden = jax.nn.gelu(
        jnp.einsum("kcm,ch->khm", column_profiles, w_in, preferred_element_type=F32)
    ).astype(jnp.bfloat16)
    if direct:
        low, high, gains = exchange_edges(
            hidden[0], hidden[-1], jnp.broadcast_to(inflation[:, None], (8, 128)), n_cols
        )
        low, high, gains = low[None], high[None], gains[:, 0, 0]
    else:
        forward = [(i, i + 1) for i in range(n_cols - 1)]
        low = lax.ppermute(hidden[-1:], "cols", forward)
        high = lax.ppermute(hidden[:1], "cols", [(t, s) for s, t in forward])
        gains = lax.all_gather(inflation, "cols", axis=0, tiled=True)
    hidden = jnp.concatenate([low, hidden, high], axis=0)
    mixed = (
        w_depth[0][None, :, None] * hidden[:-2]
        + w_depth[1][None, :, None] * hidden[1:-1]
        + w_depth[2][None, :, None] * hidden[2:]
    ).astype(jnp.bfloat16)
    forecast = column_profiles.astype(F32) + jnp.einsum(
        "khm,hc->kcm", mixed, w_out, preferred_element_type=F32
    )
    sums = jnp.sum(forecast, axis=2)
    seen = jnp.einsum("kcm,co->kom", forecast, obs_op, precision=TOP).reshape(col_dev * n_obs, mem_dev)
    if direct:
        seen_all, sums = exchange_mem(seen, sums)
    else:
        seen_all = lax.all_gather(seen, "mem", axis=0)
        sums = lax.psum(sums, "mem")
    mean = sums / members
    pert = (forecast - mean[:, :, None]).astype(jnp.bfloat16)
    pert_all = lax.all_gather(pert, "mem", axis=2, tiled=True)
    mobs = jnp.dot(mean, obs_op, precision=TOP)
    seen_all = seen_all - mobs.reshape(1, col_dev * n_obs, 1)
    seen = seen - mobs.reshape(col_dev * n_obs, 1)

    hits = (foot[:, :, None] == jnp.arange(col_dev, dtype=jnp.int32)[None, None, :]).astype(F32)
    counts = jnp.sum((foot >= 0).astype(F32), axis=1)
    onehot = jnp.sum(hits, axis=1) / counts[:, None]
    fmean = jnp.dot(onehot, mobs, precision=TOP)
    innov = (rinv * (obs - fmean)).astype(jnp.bfloat16).astype(F32)
    table = (owner == jnp.arange(n_cols, dtype=jnp.int32)[None, :]).astype(F32)
    chosen = jnp.sum(table * gains[None, :], axis=1)
    batch = foot.shape[0]
    load = (onehot[:, :, None] * (rinv * (chosen * scale)[:, None])[:, None, :]).reshape(batch, col_dev * n_obs)
    kind = jnp.arange(col_dev * n_obs, dtype=jnp.int32) % n_obs
    link = jnp.dot(load.T, load, precision=TOP) * (kind[:, None] == kind[None, :]).astype(F32)
    pull = jnp.sum(
        load * jnp.broadcast_to((innov * chosen[:, None])[:, None, :], (batch, col_dev, n_obs)).reshape(load.shape),
        axis=0,
    )
    mine = jnp.dot(link, seen, precision=TOP)
    part = jnp.einsum("qm,nqj->mnj", mine, seen_all, precision=TOP).reshape(mem_dev, members)
    vec = jnp.einsum("q,nqj->nj", pull, seen_all, precision=TOP)
    if direct:
        gram, vec = exchange_gram(part.reshape(n_cols, mem_dev // n_cols, members), vec, n_cols)
        gram = gram.reshape(members, members)
    else:
        part, vec = lax.psum((part, vec), "cols")
        gram = lax.all_gather(part, "mem", axis=0, tiled=True)
    first = lax.axis_index("mem").astype(jnp.int32)[None]
    mix = factor(first, gram, vec.reshape(1, members), mem_dev, scale)
    moved = jnp.einsum("kcm,jm->kcj", pert_all, mix, preferred_element_type=F32)
    return (mean[:, :, None] + moved).astype(jnp.bfloat16)


def solution(mesh):
    placed = (
        P("cols", None, "mem"),
        P(),
        P(),
        P(),
        P(),
        P("cols", None),
        P("cols", None),
        P("cols", None),
        P("cols", None),
        P("cols"),
    )
    return jax.shard_map(
        body, mesh=mesh, in_specs=placed, out_specs=P("cols", None, "mem"), check_vma=False
    )
```

profile of v0, /device:TPU:0, one launch (start us, length us, event | category | flops | bytes accessed | tf_op | source)
XLA Modules:
  0.0 84.7 jit_solution(15792630580237175458)
XLA Ops:
  6.5 0.0 copy-start
  6.5 0.0 copy-start.5
  6.5 0.0 copy-start.4
  6.5 0.0 copy-start.6
  6.5 0.0 all-gather.2.cloned.1.call-start
  6.6 0.8 copy-done
  7.3 1.9 %fusion.7 = bf16[16,256,128]{2,1,0:T(8,128)(2,1)S(1)} fusion(bf16[16,100,128]{2,0,1:T(8,128)(2,1)} %param.10, bf16[100,256]{1,0:T(8,128)(2,1)S(1)} %copy-done), kind=kOutput, calls=%fused_computation.8 | convolution fusion | flops 109576192 | bytes 1509376 | tf_op jit(solution)/shard_map/kcm,ch->khm/dot_general | solution.py:326
  9.9 0.0 copy-done.4
  10.0 10.3 %shard_map.100 = (bf16[256,128]{1,0:T(8,128)(2,1)S(1)}, bf16[256,128]{1,0:T(8,128)(2,1)S(1)}, f32[8,8,128]{2,1,0:T(8,128)S(1)}) custom-call(bf16[256,128]{1,0:T(8,128)(2,1)S(1)} %get-tuple-element.20.first_ref, bf16[256,128]{1,0:T(8,128)(2,1)S(1)} %get-tuple-element.19.last_ref, f32[8,128]{1,0:T(8,128)S(1)} %broadcast_in_dim.13.factor_ref), custom_call_target="tpu_custom_call" | custom-call | tf_op jit(solution)/shard_map/pallas_call | solution.py:60
  20.3 0.0 copy-done.5
  20.3 0.0 copy-done.6
  20.3 0.0 copy-start.1
  20.3 1.0 %fusion.36 = (f32[16,100]{1,0:T(8,128)S(1)}, f32[16,100,128]{2,1,0:T(8,128)S(1)}) fusion(bf16[256,100]{0,1:T(8,128)(2,1)S(1)} %copy-done.6, bf16[16,256,128]{2,1,0:T(8,128)(2,1)S(1)} %fusion.7, bf16[1,256,128]{2,1,0:T(8,128)(2,1)S(1)} %bitcast.59, bf16[1,256,128]{2,1,0:T(8,128)(2,1)S(1)} %bitcast.58, f32[256]{0:T(256)S(1)} %bitcast.63, ...), kind=kOutput, calls=%fused_computation.61 | convolution fusion | flops 111237568 | bytes 2469120 | tf_op jit(solution)/shard_map/khm,hc->kcm/dot_general | solution.py:344
  21.3 0.0 copy-start.2
  21.3 0.0 copy-start.8
  21.3 0.0 copy-start.3
  21.3 0.0 copy-start.7
  21.3 0.0 copy-done.1
  21.3 0.6 fusion.31
  21.9 7.0 %shard_map.101 = (f32[4,256,128]{2,1,0:T(8,128)S(1)}, f32[16,100]{1,0:T(8,128)S(1)}) custom-call(f32[256,128]{1,0:T(8,128)S(1)} %bitcast.54, f32[16,100]{1,0:T(8,128)S(1)} %get-tuple-element.26.sums_ref), custom_call_target="tpu_custom_call" | custom-call | tf_op jit(solution)/shard_map/pallas_call | solution.py:112
  29.0 1.0 %subtract_convert_fusion = bf16[16,100,128]{2,1,0:T(8,128)(2,1)} fusion(f32[16,100,128]{2,1,0:T(8,128)S(1)} %get-tuple-element.27, f32[16,100]{1,0:T(8,128)S(1)} %broadcast_multiply_fusion.2), kind=kLoop, calls=%fused_computation.28 | loop fusion | flops 409600 | bytes 1235200 | tf_op jit(solution)/shard_map/convert_element_type | solution.py:355
  30.0 0.0 all-gather.2.cloned.1.call-update
  30.0 0.1 fusion.34
  30.2 0.0 copy-done.2
  30.2 0.1 slice_reduce_fusion
  30.4 0.0 copy-done.8
  30.4 0.1 select_reduce_fusion
  30.5 0.1 sub.28
  30.5 0.0 copy-done.3
  30.6 0.0 copy-done.7
  30.6 0.2 fusion.13
  30.8 0.1 multiply_reduce_fusion
  30.9 0.1 reshape.88
  31.0 0.4 convolution_select_fusion
  31.4 0.5 convolution_bitcast_fusion.1
  31.8 0.5 fusion.19
  32.3 0.5 fusion.21
  32.8 0.2 copy.26
  33.0 0.1 reshape_reshape.3.part_ref
  33.1 22.4 %shard_map.102 = (f32[4,8,16,512]{3,2,1,0:T(8,128)S(1)}, f32[4,128]{1,0:T(4,128)S(1)}) custom-call(f32[8,16,512]{2,1,0:T(8,128)S(1)} %reshape_reshape.3.part_ref, f32[4,128]{1,0:T(4,128)S(1)} %bitcast.56), custom_call_target="tpu_custom_call" | custom-call | tf_op jit(solution)/shard_map/pallas_call | solution.py:201
  55.5 19.5 %shard_map.103 = bf16[128,512]{1,0:T(8,128)(2,1)S(1)} custom-call(s32[1]{0:T(128)} %bitcast.16.first_ref, f32[512,512]{1,0:T(8,128)S(1)} %bitcast.57, f32[1,512]{1,0:T(1,128)S(1)} %bitcast.60), custom_call_target="tpu_custom_call" | custom-call | flops 40000000000 | bytes 4194304 | tf_op jit(solution)/shard_map/pallas_call | solution.py:305
  75.0 0.0 all-gather.2.cloned.1.call-done
  75.0 2.1 %fusion.9 = bf16[16,100,128]{2,1,0:T(8,128)(2,1)S(1)} fusion(bf16[16,100,512]{2,1,0:T(8,128)(2,1)} %all-gather.2.cloned.1.call-done, f32[16,100]{1,0:T(8,128)S(1)} %broadcast_multiply_fusion.2, bf16[128,512]{1,0:T(8,128)(2,1)S(1)} %shard_map.103), kind=kOutput, calls=%fused_computation.13 | convolution fusion | flops 210124800 | bytes 2185472 | tf_op jit(solution)/shard_map/kcm,jm->kcj/dot_general | solution.py:387
  77.1 0.8 copy.27
  (9 shorter events, 0.1 us)
Async XLA Ops:
  6.5 0.8 copy-start
  6.5 13.7 %copy-start.5 = (bf16[16,100,128]{2,0,1:T(8,128)(2,1)S(1)}, bf16[16,100,128]{2,0,1:T(8,128)(2,1)}, u32[]{:S(2)}) copy-start(bf16[16,100,128]{2,0,1:T(8,128)(2,1)} %param.10) | copy-start | bytes 1228804
  6.5 3.4 %copy-start.4 = (f32[3,256]{1,0:T(4,128)S(1)}, f32[3,256]{1,0:T(4,128)}, u32[]{:S(2)}) copy-start(f32[3,256]{1,0:T(4,128)} %param.12) | copy-start | bytes 9220
  6.5 13.8 %copy-start.6 = (bf16[256,100]{0,1:T(8,128)(2,1)S(1)}, bf16[256,100]{0,1:T(8,128)(2,1)}, u32[]{:S(2)}) copy-start(bf16[256,100]{0,1:T(8,128)(2,1)} %param.13) | copy-start | bytes 153604
  6.5 68.4 %all-gather.2.cloned.1.call-start = ((), (), s32[]{:S(2)}) async-start(), calls=%async_computation | async-start | bytes 2129920 | tf_op jit(solution)/shard_map/all_gather | solution.py:356
  20.3 1.0 %copy-start.1 = (f32[100,16]{0,1:T(8,128)S(1)}, f32[100,16]{0,1:T(8,128)}, u32[]{:S(2)}) copy-start(f32[100,16]{0,1:T(8,128)} %param.14) | copy-start | bytes 19204
  21.3 8.9 %copy-start.2 = (s32[128,4]{0,1:T(4,128)S(1)}, s32[128,4]{0,1:T(4,128)}, u32[]{:S(2)}) copy-start(s32[128,4]{0,1:T(4,128)} %param.15) | copy-start | bytes 6148
  21.3 9.1 %copy-start.8 = (s32[128,1]{0,1:T(1,128)S(1)}, s32[128,1]{0,1:T(1,128)}, u32[]{:S(2)}) copy-start(s32[128,1]{0,1:T(1,128)} %param.16) | copy-start | bytes 1540
  21.3 9.2 %copy-start.3 = (f32[128,16]{0,1:T(8,128)S(1)}, f32[128,16]{0,1:T(8,128)}, u32[]{:S(2)}) copy-start(f32[128,16]{0,1:T(8,128)} %param.18) | copy-start | bytes 24580
  21.3 9.2 %copy-start.7 = (f32[128,16]{0,1:T(8,128)S(1)}, f32[128,16]{0,1:T(8,128)}, u32[]{:S(2)}) copy-start(f32[128,16]{0,1:T(8,128)} %param.17) | copy-start | bytes 24580
Sparse Core Ops, SparseCore 0:
  30.2 20.7 all-gather.1
where the time goes:
time: 84.9 us; the launch traced here: 84.7 us
  Pallas kernels  59.2 us (70%)
  between operations  14.3 us (17%)
  matrix products  7.68 us (9%)
  local copies, waits for them, and re-layouts  2.21 us (3%)
  other arithmetic  1.29 us (2%)
    pallas_call x1, Pallas kernels, exchange_gram(): pl.pallas_call(functools.partial(gram_kernel, n_cols), out_shape=(jax.Sha...  22.4 us
    pallas_call x1, Pallas kernels, factor(): pl.pallas_call(functools.partial(factor_kernel, scale), out_shape=jax.Sha...  19.5 us
    pallas_call x1, Pallas kernels, exchange_edges(): pl.pallas_call(functools.partial(edge_kernel, n_cols), out_shape=(jax.Sha...  10.3 us
    pallas_call x1, Pallas kernels, exchange_mem(): pl.pallas_call(mem_kernel, out_shape=(jax.ShapeDtypeStruct((4,) + seen.sh...  7.01 us
    dot_general x1, matrix products, body(): moved = jnp.einsum('kcm,jm->kcj', pert_all, mix, preferred_element_type=F32)  2.06 us
    dot_general x1, matrix products, body(): jnp.einsum('kcm,ch->khm', column_profiles, w_in, preferred_element_type=F32)  1.92 us
  transfers between devices with their start and end apart: 1, of which 0 were waited for; matrix products, arithmetic and copies ran while one was open for 4% of the time, Pallas kernels for 49%

commit v1 on v0

--- a/solution.py
+++ b/solution.py
@@ -98,14 +98,15 @@
         t = remote(buf.at[0], buf.at[2], send.at[i, 2], recv.at[i, 2], {"mem": near})
         t.start()
         thirds.append(t)
-    all_ref[m] = seen_ref[...]
-    all_ref[far] = seen_buf[0]
+    all_ref[0] = seen_ref[...]
+    all_ref[2] = seen_buf[0]
     for i in range(2):
         copies[i][1].wait()
         thirds[i].wait()
     total_ref[...] = (sums_ref[...] + sums_buf[0]) + (sums_buf[1] + sums_buf[2])
-    all_ref[near] = seen_buf[1]
-    all_ref[lax.rem(near + 2, 4)] = seen_buf[2]
+    turn = lax.rem(near - m + 4, 4)
+    all_ref[turn] = seen_buf[1]
+    all_ref[4 - turn] = seen_buf[2]
 
 
 def exchange_mem(seen, sums):
@@ -127,7 +128,8 @@
     )(seen, sums)
 
 
-def gram_kernel(n_cols, part_ref, vec_ref, gram_ref, total_ref, rbuf, vbuf, gbuf,
+def gram_kernel(n_cols, part_ref, vec_ref, pert_ref, gram_ref, total_ref, others_ref, rbuf, vbuf, gbuf, pbuf,
+                p_send, p_recv,
                 r_send, r_recv, v_send, v_recv, g_send, g_recv,
                 a_send, a_recv, b_send, b_recv, t_send, t_recv):
     c = lax.axis_index("cols")
@@ -144,6 +146,10 @@
         copy = remote(part_ref.at[peer], rbuf.at[d - 1], r_send.at[d - 1], r_recv.at[d - 1], {"cols": peer})
         copy.start()
         rows.append(copy)
+    pert_far = remote(pert_ref, pbuf.at[0], p_send.at[0], p_recv.at[0], {"mem": far})
+    pert_near = remote(pert_ref, pbuf.at[1], p_send.at[1], p_recv.at[1], {"mem": near})
+    pert_far.start()
+    pert_near.start()
     for d in range(1, n_cols):
         peer = lax.rem(c + d, n_cols)
         copy = remote(vec_ref, vbuf.at[d - 1], v_send.at[d - 1], v_recv.at[d - 1], {"cols": peer})
@@ -170,6 +176,9 @@
         a.start()
         b.start()
         pairs.append((a, b))
+    pert_far.wait()
+    pert_third = remote(pbuf.at[0], pbuf.at[2], p_send.at[2], p_recv.at[2], {"mem": near})
+    pert_third.start()
     thirds = []
     for d in range(n_cols):
         held = lax.rem(c + n_cols - d, n_cols)
@@ -181,7 +190,8 @@
     for d in range(1, n_cols):
         vecs[d - 1].wait()
         whole = whole + vbuf[d - 1]
-    total_ref[...] = whole
+    for i in range(4):
+        total_ref[lax.rem(m + i, 4)] = whole[i]
     for d in range(n_cols):
         pairs[d][1].wait_recv()
         thirds[d].wait_recv()
@@ -192,9 +202,12 @@
         pairs[d][1].wait_send()
         thirds[d].wait_send()
     gram_ref[...] = gbuf[...]
-
-
-def exchange_gram(part, vec, n_cols):
+    pert_near.wait()
+    pert_third.wait()
+    others_ref[...] = pbuf[...]
+
+
+def exchange_gram(part, vec, pert, n_cols):
     count = n_cols - 1
     dma = pltpu.SemaphoreType.DMA
     slab = part.shape[1:]
@@ -203,16 +216,20 @@
         out_shape=(
             jax.ShapeDtypeStruct((4, n_cols) + slab, F32),
             jax.ShapeDtypeStruct(vec.shape, F32),
+            jax.ShapeDtypeStruct((3,) + pert.shape, pert.dtype),
         ),
-        in_specs=[VMEM] * 2,
-        out_specs=(VMEM,) * 2,
+        in_specs=[VMEM] * 3,
+        out_specs=(VMEM,) * 3,
         scratch_shapes=[
             pltpu.VMEM((count,) + slab, F32),
             pltpu.VMEM((count,) + vec.shape, F32),
             pltpu.VMEM((4, n_cols) + slab, F32),
+            pltpu.VMEM((3,) + pert.shape, pert.dtype),
+            dma((3,)),
+            dma((3,)),
         ] + [dma((count,))] * 6 + [dma((n_cols,))] * 6,
         compiler_params=pltpu.CompilerParams(collective_id=2, has_side_effects=True, vmem_limit_bytes=16 << 20),
-    )(part, vec)
+    )(part, vec, pert)
 
 
 def lane_copy(x, j):
@@ -250,11 +267,22 @@
     return block
 
 
-def factor_kernel(scale, first_ref, gram_ref, vec_ref, mix_ref, w_ref):
+def factor_kernel(scale, first_ref, gram_ref, vec_ref, *rest):
+    if len(rest) == 6:
+        pert_ref, others_ref, mean_ref, out_ref, w_ref, mix_ref = rest
+    else:
+        pert_ref, (mix_ref, w_ref) = None, rest
     width = 128
-    order = gram_ref.shape[0]
+    order = w_ref.shape[0]
     blocks = order // width
-    w_ref[...] = gram_ref[...]
+    if len(gram_ref.shape) == 2:
+        w_ref[...] = gram_ref[...]
+    else:
+        for r in range(4):
+            for t in range(min(3, 4 - r)):
+                at = (r + t) * width
+                w_ref[r * width:(r + 1) * width, at:at + width] = gram_ref[r, :, t * width:(t + 1) * width]
+        w_ref[0:width, 3 * width:] = gram_ref[3, :, width:2 * width].T
     lane = lax.broadcasted_iota(jnp.int32, (8, width), 1)
     sub = lax.broadcasted_iota(jnp.int32, (8, width), 0)
 
@@ -298,10 +326,37 @@
     weights = jnp.sum(chol_inverse * half, axis=0, keepdims=True)
     mine = w_ref[pl.ds(pl.multiple_of(first_ref[0] * width, width), mix_ref.shape[0]), :]
     mix_ref[...] = (weights * scale + mine).astype(mix_ref.dtype)
+    if pert_ref is None:
+        return
+    m = first_ref[0]
+    near = m + 1 - 2 * lax.rem(m, 2)
+    sources = ((pert_ref[...], m), (others_ref[0], lax.rem(m + 2, 4)), (others_ref[1], near), (others_ref[2], lax.rem(near + 2, 4)))
+    moved = None
+    for source, place in sources:
+        weight = mix_ref[:, pl.ds(pl.multiple_of(place * width, width), width)]
+        term = lax.dot_general(source, weight, (((1,), (1,)), ((), ())), preferred_element_type=F32)
+        moved = term if moved is None else moved + term
+    mean = mean_ref[...]
+    col_dev = mean.shape[0]
+    for c in range(mean.shape[1]):
+        out_ref[c] = (moved[c * col_dev:(c + 1) * col_dev] + mean[:, c:c + 1]).astype(out_ref.dtype)
+
+
+def analyse(first, gram, vec, pert, others, mean, rows, scale):
+    order = vec.shape[1]
+    col_dev, channels = mean.shape
+    return pl.pallas_call(
+        functools.partial(factor_kernel, scale),
+        out_shape=jax.ShapeDtypeStruct((channels, col_dev, rows), jnp.bfloat16),
+        in_specs=[pl.BlockSpec(memory_space=pltpu.SMEM)] + [VMEM] * 5,
+        out_specs=VMEM,
+        scratch_shapes=[pltpu.VMEM((order, order), F32), pltpu.VMEM((rows, order), jnp.bfloat16)],
+        compiler_params=pltpu.CompilerParams(vmem_limit_bytes=32 << 20),
+    )(first, gram, vec, pert, others, mean)
 
 
 def factor(first, gram, vec, rows, scale):
-    order = gram.shape[0]
+    order = vec.shape[1]
     return pl.pallas_call(
         functools.partial(factor_kernel, scale),
         out_shape=jax.ShapeDtypeStruct((rows, order), jnp.bfloat16),
@@ -319,7 +374,7 @@
     col_dev, channels, mem_dev = column_profiles.shape
     n_obs = obs.shape[1]
     members = mem_dev * n_mem
-    direct = n_cols <= 8 and n_mem == 4
+    direct = n_cols <= 8 and n_mem == 4 and mem_dev == 128
     scale = 1.0 / math.sqrt(members - 1)
 
     hidden = jax.nn.gelu(
@@ -353,7 +408,10 @@
         sums = lax.psum(sums, "mem")
     mean = sums / members
     pert = (forecast - mean[:, :, None]).astype(jnp.bfloat16)
-    pert_all = lax.all_gather(pert, "mem", axis=2, tiled=True)
+    if direct:
+        pert = jnp.transpose(pert, (1, 0, 2)).reshape(channels * col_dev, mem_dev)
+    else:
+        pert_all = lax.all_gather(pert, "mem", axis=2, tiled=True)
     mobs = jnp.dot(mean, obs_op, precision=TOP)
     seen_all = seen_all - mobs.reshape(1, col_dev * n_obs, 1)
     seen = seen - mobs.reshape(col_dev * n_obs, 1)
@@ -374,15 +432,19 @@
         axis=0,
     )
     mine = jnp.dot(link, seen, precision=TOP)
-    part = jnp.einsum("qm,nqj->mnj", mine, seen_all, precision=TOP).reshape(mem_dev, members)
+    used = seen_all[:3] if direct else seen_all
+    part = jnp.einsum("qm,nqj->mnj", mine, used, precision=TOP).reshape(mem_dev, -1)
     vec = jnp.einsum("q,nqj->nj", pull, seen_all, precision=TOP)
     if direct:
-        gram, vec = exchange_gram(part.reshape(n_cols, mem_dev // n_cols, members), vec, n_cols)
-        gram = gram.reshape(members, members)
+        gram, vec, others = exchange_gram(part.reshape(n_cols, mem_dev // n_cols, -1), vec, pert, n_cols)
+        gram = gram.reshape(n_mem, mem_dev, -1)
     else:
         part, vec = lax.psum((part, vec), "cols")
         gram = lax.all_gather(part, "mem", axis=0, tiled=True)
     first = lax.axis_index("mem").astype(jnp.int32)[None]
+    if direct:
+        out = analyse(first, gram, vec.reshape(1, members), pert, others, mean, mem_dev, scale)
+        return jnp.transpose(out, (1, 0, 2))
     mix = factor(first, gram, vec.reshape(1, members), mem_dev, scale)
     moved = jnp.einsum("kcm,jm->kcj", pert_all, mix, preferred_element_type=F32)
     return (mean[:, :, None] + moved).astype(jnp.bfloat16)

time: 84.9 us -> 68.7 us (0.81)
  between operations: 14.3 us -> 0.86 us
  matrix products: 7.68 us -> 5.44 us
    dot_general x2 -> x1, matrix products: 2.59 us -> 0.39 us  [body(): jnp.einsum('qm,nqj->mnj', mine, used, precision=TOP).reshape(mem_dev, -1)]
    pallas_call x1, Pallas kernels: 22.4 us -> 20.4 us  [exchange_gram(): pl.pallas_call(functools.partial(gram_kernel, n_cols), out_shape=(jax.Sha...]
    pallas_call x1, Pallas kernels: 19.5 us -> 20.9 us  [analyse(): pl.pallas_call(functools.partial(factor_kernel, scale), out_shape=jax.Sha...]
    convert_element_type x1 -> x0, other arithmetic: 1.04 us -> none  [body(): pert = (forecast - mean[:, :, None]).astype(jnp.bfloat16)]
  transfers between devices with their start and end apart: 1 -> 0, of which waited for: 0 -> 0; matrix products, arithmetic and copies ran while one was open for 4% -> 0% of each run, Pallas kernels for 49% -> 0%
where the time goes in v1:
time: 68.7 us; the launch traced here: 68.4 us
  Pallas kernels  58.6 us (85%)
  matrix products  5.44 us (8%)
  other arithmetic  2.01 us (3%)
  local copies, waits for them, and re-layouts  1.46 us (2%)
  between operations  0.86 us (1%)
    pallas_call x1, Pallas kernels, analyse(): pl.pallas_call(functools.partial(factor_kernel, scale), out_shape=jax.Sha...  20.9 us
    pallas_call x1, Pallas kernels, exchange_gram(): pl.pallas_call(functools.partial(gram_kernel, n_cols), out_shape=(jax.Sha...  20.4 us
    pallas_call x1, Pallas kernels, exchange_edges(): pl.pallas_call(functools.partial(edge_kernel, n_cols), out_shape=(jax.Sha...  10.3 us
    pallas_call x1, Pallas kernels, exchange_mem(): pl.pallas_call(mem_kernel, out_shape=(jax.ShapeDtypeStruct((4,) + seen.sh...  7.02 us
    dot_general x1, matrix products, body(): jnp.einsum('kcm,ch->khm', column_profiles, w_in, preferred_element_type=F32)  1.97 us

profile of v1, /device:TPU:0, one launch (start us, length us, event | category | flops | bytes accessed | tf_op | source)
XLA Modules:
  0.0 68.4 jit_solution(6711769888972638864)
XLA Ops:
  0.0 0.0 copy-start
  0.7 0.7 %convert_reduce_fusion.1 = f32[128]{0:T(128)S(1)} fusion(s32[128,4]{0,1:T(4,128)} %param.15), kind=kLoop, calls=%fused_computation.50 | loop fusion | flops 1408 | bytes 2560 | tf_op jit(solution)/shard_map/reduce_sum | solution.py:420
  1.4 0.8 %fusion.30 = (f32[1,256]{1,0:T(1,128)S(1)}, f32[1,256]{1,0:T(1,128)S(1)}, f32[1,256]{1,0:T(1,128)S(1)}) fusion(f32[3,256]{1,0:T(4,128)} %param.12), kind=kLoop, calls=%fused_computation.55 | loop fusion | bytes 6144 | tf_op jit(solution)/shard_map/slice | solution.py:395
  2.2 0.7 %convert_reduce_fusion = f32[128,16]{0,1:T(8,128)S(1)} fusion(s32[128,4]{0,1:T(4,128)} %param.15), kind=kLoop, calls=%fused_computation.40 | loop fusion | flops 22528 | bytes 10240 | tf_op jit(solution)/shard_map/reduce_sum | solution.py:421
  2.9 0.0 copy-done
  2.9 0.0 copy-start.6
  2.9 0.0 copy-start.3
  2.9 0.0 copy-start.4
  2.9 2.0 %fusion.7 = bf16[16,256,128]{2,1,0:T(8,128)(2,1)S(1)} fusion(bf16[16,100,128]{2,0,1:T(8,128)(2,1)} %param.10, bf16[100,256]{1,0:T(8,128)(2,1)S(1)} %copy-done), kind=kOutput, calls=%fused_computation.8 | convolution fusion | flops 109576192 | bytes 1509376 | tf_op jit(solution)/shard_map/kcm,ch->khm/dot_general | solution.py:381
  4.9 10.3 %shard_map.100 = (bf16[256,128]{1,0:T(8,128)(2,1)S(1)}, bf16[256,128]{1,0:T(8,128)(2,1)S(1)}, f32[8,8,128]{2,1,0:T(8,128)S(1)}) custom-call(bf16[256,128]{1,0:T(8,128)(2,1)S(1)} %get-tuple-element.22.first_ref, bf16[256,128]{1,0:T(8,128)(2,1)S(1)} %get-tuple-element.21.last_ref, f32[8,128]{1,0:T(8,128)S(1)} %broadcast_in_dim.14.factor_ref), custom_call_target="tpu_custom_call" | custom-call | tf_op jit(solution)/shard_map/pallas_call | solution.py:60
  15.2 0.1 slice_reduce_fusion
  15.4 0.0 copy-done.6
  15.4 0.1 select_reduce_fusion
  15.4 0.0 copy-done.3
  15.4 0.0 copy-done.4
  15.4 0.0 copy-start.2
  15.5 0.0 copy-start.1
  15.5 1.0 %fusion.31 = (f32[16,100]{1,0:T(8,128)S(1)}, f32[16,100,128]{2,1,0:T(8,128)S(1)}) fusion(bf16[256,100]{0,1:T(8,128)(2,1)S(1)} %copy-done.4, bf16[16,256,128]{2,1,0:T(8,128)(2,1)S(1)} %fusion.7, bf16[1,256,128]{2,1,0:T(8,128)(2,1)S(1)} %bitcast.63, bf16[1,256,128]{2,1,0:T(8,128)(2,1)S(1)} %bitcast.62, f32[256]{0:T(256)S(1)} %bitcast.66, ...), kind=kOutput, calls=%fused_computation.56 | convolution fusion | flops 111237568 | bytes 2469120 | tf_op jit(solution)/shard_map/khm,hc->kcm/dot_general | solution.py:399
  16.4 0.0 copy-done.2
  16.5 0.0 copy-done.1
  16.5 0.6 fusion.26
  17.1 0.0 copy-start.5
  17.1 7.0 %shard_map.101 = (f32[4,256,128]{2,1,0:T(8,128)S(1)}, f32[16,100]{1,0:T(8,128)S(1)}) custom-call(f32[256,128]{1,0:T(8,128)S(1)} %bitcast.57, f32[16,100]{1,0:T(8,128)S(1)} %get-tuple-element.28.sums_ref), custom_call_target="tpu_custom_call" | custom-call | tf_op jit(solution)/shard_map/pallas_call | solution.py:113
  24.1 0.1 fusion.29
  24.2 0.3 fusion.18
  24.6 0.1 copy.27
  24.6 0.1 sub.29
  24.7 0.0 copy-done.5
  24.7 0.2 fusion.12
  24.9 0.1 broadcast_subtract_fusion
  25.0 0.1 multiply_reduce_fusion
  25.1 0.1 reshape.92
  25.2 0.4 fusion.32
  25.6 0.4 convolution_select_fusion
  26.0 0.5 convolution_bitcast_fusion.1
  26.4 0.4 fusion.19
  26.8 0.1 copy.26
  27.0 0.1 reshape_reshape.3.part_ref
  27.1 20.4 %shard_map.102 = (f32[4,8,16,384]{3,2,1,0:T(8,128)S(1)}, f32[4,128]{1,0:T(4,128)S(1)}, bf16[3,1600,128]{2,1,0:T(8,128)(2,1)S(1)}) custom-call(f32[8,16,384]{2,1,0:T(8,128)S(1)} %reshape_reshape.3.part_ref, f32[4,128]{1,0:T(4,128)S(1)} %bitcast.60, bf16[1600,128]{1,0:T(8,128)(2,1)S(1)} %bitcast.55), custom_call_target="tpu_custom_call" | custom-call | tf_op jit(solution)/shard_map/pallas_call | solution.py:214
  47.5 20.9 %shard_map.103 = bf16[100,16,128]{2,1,0:T(8,128)(2,1)} custom-call(s32[1]{0:T(128)} %bitcast.16.first_ref, f32[4,128,384]{2,1,0:T(8,128)S(1)} %bitcast.59, f32[1,512]{1,0:T(1,128)S(1)} %bitcast.61, bf16[1600,128]{1,0:T(8,128)(2,1)S(1)} %bitcast.56, bf16[3,1600,128]{2,1,0:T(8,128)(2,1)S(1)} %get-tuple-element.20.rest_1_, ...), custom_call_target="tpu_custom_call" | custom-call | tf_op jit(solution)/shard_map/pallas_call | solution.py:348
  (6 shorter events, 0.0 us)
Async XLA Ops:
  0.0 2.9 %copy-start = (bf16[100,256]{1,0:T(8,128)(2,1)S(1)}, bf16[100,256]{1,0:T(8,128)(2,1)}, u32[]{:S(2)}) copy-start(bf16[100,256]{1,0:T(8,128)(2,1)} %param.11) | copy-start | bytes 153604
  2.9 12.5 %copy-start.6 = (s32[128,1]{0,1:T(1,128)S(1)}, s32[128,1]{0,1:T(1,128)}, u32[]{:S(2)}) copy-start(s32[128,1]{0,1:T(1,128)} %param.16) | copy-start | bytes 1540
  2.9 12.6 %copy-start.3 = (bf16[16,100,128]{2,0,1:T(8,128)(2,1)S(1)}, bf16[16,100,128]{2,0,1:T(8,128)(2,1)}, u32[]{:S(2)}) copy-start(bf16[16,100,128]{2,0,1:T(8,128)(2,1)} %param.10) | copy-start | bytes 1228804
  2.9 12.6 %copy-start.4 = (bf16[256,100]{0,1:T(8,128)(2,1)S(1)}, bf16[256,100]{0,1:T(8,128)(2,1)}, u32[]{:S(2)}) copy-start(bf16[256,100]{0,1:T(8,128)(2,1)} %param.13) | copy-start | bytes 153604
  15.4 1.0 %copy-start.2 = (f32[128,16]{0,1:T(8,128)S(1)}, f32[128,16]{0,1:T(8,128)}, u32[]{:S(2)}) copy-start(f32[128,16]{0,1:T(8,128)} %param.18) | copy-start | bytes 24580
  15.5 1.0 %copy-start.1 = (f32[100,16]{0,1:T(8,128)S(1)}, f32[100,16]{0,1:T(8,128)}, u32[]{:S(2)}) copy-start(f32[100,16]{0,1:T(8,128)} %param.14) | copy-start | bytes 19204
  17.1 7.6 %copy-start.5 = (f32[128,16]{0,1:T(8,128)S(1)}, f32[128,16]{0,1:T(8,128)}, u32[]{:S(2)}) copy-start(f32[128,16]{0,1:T(8,128)} %param.17) | copy-start | bytes 24580
